TPU v7x, 512 devices: a whole 4x8x8 slice. The times are simulated.
512 devices in a mesh: dom: 128 (over z, y, core), sub: 4 (over x).
Axes of the slice: x: 4, y: 8, z: 8, core: 2. Of those that a mesh axis runs over, the one named last changes fastest.
Arguments:
- rhs: float32 [64, 8, 65536], P(None, None, ('dom', 'sub')), may hold values from -6 to 6
- guess: float32 [64, 8, 65536], P(None, None, ('dom', 'sub')), may hold values from -4 to 4
- diag_blocks: bfloat16 [2, 64, 64], replicated
- face_blocks: bfloat16 [6, 2, 64, 64], replicated, may hold values from -0.3125 to 0.3125
- smoother: bfloat16 [2, 64, 64], replicated
- coarse_inverse: bfloat16 [64, 64], replicated
- elem_type: int32 [65536], P(('dom', 'sub')), may hold values from 0 to 1
- face_type: int32 [6, 65536], P(None, ('dom', 'sub')), may hold values from 0 to 1
- neighbours: int32 [6, 65536], P(None, ('dom', 'sub')), may hold values from 0 to 239, as said below
- send_near: int32 [2, 16384], P(None, ('dom', 'sub')), may hold values from 0 to 127
- send_far: int32 [2, 4096], P(None, ('dom', 'sub')), may hold values from 0 to 127
- sub_send: int32 [4096], P(('dom', 'sub')), may hold values from 0 to 127
- partner: int32 [65536], P(('dom', 'sub')), may hold values from 0 to 143, as said below
- pair_send: int32 [8192], P(('dom', 'sub')), may hold values from 0 to 127, as said below
Outputs:
- solution: float32 [64, 8, 65536], P(None, None, ('dom', 'sub'))
- residual: float32 [64, 8, 65536], P(None, None, ('dom', 'sub'))
Inputs may be any that keep to these rules, and one draw needn't show every extreme that they name: `neighbours`: values below 128 are the device's own elements; the rest index its 112 received rows in the order of the first step. On each device the partner relation is mutual: local values pair two distinct local elements with each other; each value 128 + q for q below 16 appears exactly once, and the element holding it is entry q of the device's pair_send. `pair_send`: on each device the 16 entries are distinct; slot q pairs with slot q of the device whose sub index differs in the lowest bit.
All inputs are finite; a program needn't handle non-finite values.
Results may differ from a plain program's by a relative error of at most 0.012.
Values may be sent and summed in bfloat16 or wider, within the bound.
No kernel may reach another device: no remote copies, remote signals or barrier semaphores. Data moves between devices by JAX's collectives and lax.ppermute only.
A program may use at most 64 MiB of HBM per device.

v0:
```python
import jax
import jax.numpy as jnp
from jax import lax
from jax.sharding import PartitionSpec as P

SWEEPS = 2


def from_behind(array, axis, by):
    peers = lax.axis_size(axis)
    pairs = [(i, i + by) for i in range(peers) if 0 <= i + by < peers]
    return lax.ppermute(array, axis, pairs)


def partner_2(block, axis, stride):
    count = lax.axis_size(axis)
    route = []
    for low in range(count):
        high = low | 1 << stride
        if high != low and high < count:
            route += [(low, high), (high, low)]
    return lax.ppermute(block, axis, route)


def stack_apply(blocks, field_b, kinds):
    variants = blocks.shape[0]
    node_rows, rhs_width, elements = field_b.shape
    blank = jnp.zeros_like(field_b)
    pieces = [
        jnp.where(kinds[None, None, :] == variant, field_b, blank) for variant in range(variants)
    ]
    operand = jnp.concatenate(pieces, axis=0).reshape(variants * node_rows, rhs_width * elements)
    wide_blocks = jnp.concatenate([blocks[variant] for variant in range(variants)], axis=1)
    product = jnp.dot(wide_blocks, operand, preferred_element_type=jnp.float32)
    return product.reshape(node_rows, rhs_width, elements)


def body(
    rhs,
    guess,
    diag_blocks,
    face_blocks,
    smoother,
    coarse_inverse,
    elem_type,
    face_type,
    neighbours,
    send_near,
    send_far,
    sub_send,
    partner,
    pair_send,
):

    def apply_local(field_b):
        up_near = jnp.take(field_b, send_near[1], axis=2)
        down_near = jnp.take(field_b, send_near[0], axis=2)
        up_far = jnp.take(field_b, send_far[1], axis=2)
        down_far = jnp.take(field_b, send_far[0], axis=2)
        from_below = from_behind(up_near, "dom", 1)
        from_above = from_behind(down_near, "dom", -1)
        far_below = from_behind(up_far, "dom", 2)
        far_above = from_behind(down_far, "dom", -2)
        side_rows = lax.all_gather(jnp.take(field_b, sub_send, axis=2), "sub", axis=2, tiled=True)
        extended = jnp.concatenate(
            [field_b, from_below, from_above, far_below, far_above, side_rows], axis=2
        )
        total = stack_apply(diag_blocks, field_b, elem_type)
        for face_index in range(6):
            beside = jnp.take(extended, neighbours[face_index], axis=2)
            total = total + stack_apply(face_blocks[face_index], beside, face_type[face_index])
        return total

    iterate = guess
    for rounds in range(SWEEPS):
        sweep_res = rhs - apply_local(iterate.astype(jnp.bfloat16))
        iterate = iterate + stack_apply(smoother, sweep_res.astype(jnp.bfloat16), elem_type)
    residual = rhs - apply_local(iterate.astype(jnp.bfloat16))
    outgoing = jnp.take(residual, pair_send, axis=2)
    incoming = partner_2(outgoing.astype(jnp.bfloat16), "sub", 0).astype(outgoing.dtype)
    joined = jnp.concatenate([residual, incoming], axis=2)
    coarse = residual + jnp.take(joined, partner, axis=2)
    node_rows, rhs_width, elements = coarse.shape
    coarse_b = coarse.astype(jnp.bfloat16).reshape(node_rows, rhs_width * elements)
    update = jnp.dot(coarse_inverse, coarse_b, preferred_element_type=jnp.float32)
    solution = iterate + update.reshape(node_rows, rhs_width, elements)
    return (solution, residual)


def solution(mesh):
    in_specs = (
        P(None, None, ("dom", "sub")),
        P(None, None, ("dom", "sub")),
        P(),
        P(),
        P(),
        P(),
        P(("dom", "sub")),
        P(None, ("dom", "sub")),
        P(None, ("dom", "sub")),
        P(None, ("dom", "sub")),
        P(None, ("dom", "sub")),
        P(("dom", "sub")),
        P(("dom", "sub")),
        P(("dom", "sub")),
    )
    out_specs = (P(None, None, ("dom", "sub")), P(None, None, ("dom", "sub")))
    return jax.shard_map(body, mesh=mesh, in_specs=in_specs, out_specs=out_specs, check_vma=False)
```

profile of v0, /device:TPU:256, one launch (start us, length us, event | category | flops | bytes accessed | tf_op | source)
XLA Modules:
  0.0 147.1 jit_solution(16618105193743809623)
XLA Ops:
  0.7 0.7 broadcast_compare_fusion
  1.3 1.0 broadcast_select_fusion.27
  2.6 0.6 gather_fusion.2
  3.3 1.9 %collective-permute-start = (bf16[64,8,32]{2,0,1:T(8,128)(2,1)S(1)}, bf16[64,8,32]{2,0,1:T(8,128)(2,1)S(1)}, u32[]{:S(2)}, u32[]{:S(2)}) collective-permute-start(bf16[64,8,32]{2,0,1:T(8,128)(2,1)S(1)} %select_bitcast_fusion.5), channel_id=1, source_target_pairs={{0,4},{4,8},{8,12},{12,16},{16,20},{20,24},{24,28},{28,32},{32,36}... | collective-permute-start | bytes 98312 | tf_op jit(solution)/shard_map/ppermute | solution.py:12
  5.3 0.6 gather_fusion.3
  6.1 7.0 %collective-permute-start.1 = (bf16[64,8,32]{2,0,1:T(8,128)(2,1)S(1)}, bf16[64,8,32]{2,0,1:T(8,128)(2,1)S(1)}, u32[]{:S(2)}, u32[]{:S(2)}) collective-permute-start(bf16[64,8,32]{2,0,1:T(8,128)(2,1)S(1)} %select_bitcast_fusion.4), channel_id=1, source_target_pairs={{4,0},{8,4},{12,8},{16,12},{20,16},{24,20},{28,24},{32,28},{36,32}... | collective-permute-start | bytes 98312 | tf_op jit(solution)/shard_map/ppermute | solution.py:12
  13.7 1.9 %collective-permute-start.2 = (bf16[64,8,8]{0,1,2:T(8,128)(2,1)S(1)}, bf16[64,8,8]{0,1,2:T(8,128)(2,1)S(1)}, u32[]{:S(2)}, u32[]{:S(2)}) collective-permute-start(bf16[64,8,8]{0,1,2:T(8,128)(2,1)S(1)} %select_bitcast_fusion.14), channel_id=1, source_target_pairs={{0,8},{4,12},{8,16},{12,20},{16,24},{20,28},{24,32},{28,36},{32,40... | collective-permute-start | bytes 24584 | tf_op jit(solution)/shard_map/ppermute | solution.py:12
  16.3 7.2 %collective-permute-start.3 = (bf16[64,8,8]{0,1,2:T(8,128)(2,1)S(1)}, bf16[64,8,8]{0,1,2:T(8,128)(2,1)S(1)}, u32[]{:S(2)}, u32[]{:S(2)}) collective-permute-start(bf16[64,8,8]{0,1,2:T(8,128)(2,1)S(1)} %select_bitcast_fusion.13), channel_id=1, source_target_pairs={{8,0},{12,4},{16,8},{20,12},{24,16},{28,20},{32,24},{36,28},{40,32... | collective-permute-start | bytes 24584 | tf_op jit(solution)/shard_map/ppermute | solution.py:12
  25.6 12.2 %all_gather.9 = bf16[64,8,32]{0,1,2:T(8,128)(2,1)S(1)} all-gather(bf16[64,8,8]{0,1,2:T(8,128)(2,1)S(1)} %select_bitcast_fusion.12), channel_id=1, replica_groups=mesh['dom'=128,'sub'=4] {'sub'}, dimensions={2}, use_global_device_ids=true | all-gather | bytes 40960 | tf_op jit(solution)/shard_map/all_gather | solution.py:64
  38.8 0.7 gather_fusion.7
  40.0 0.7 gather_fusion.8
  41.1 0.7 gather_fusion.9
  42.2 0.7 gather_fusion.10
  43.4 0.7 gather_fusion.11
  44.5 0.7 gather_fusion.12
  47.0 0.7 copy-done.1
  48.2 0.7 copy-done.2
  49.4 0.6 gather_fusion.13
  50.0 0.6 gather_fusion.14
  52.9 1.9 %collective-permute-start.4 = (bf16[64,8,32]{2,0,1:T(8,128)(2,1)S(1)}, bf16[64,8,32]{2,0,1:T(8,128)(2,1)S(1)}, u32[]{:S(2)}, u32[]{:S(2)}) collective-permute-start(bf16[64,8,32]{2,0,1:T(8,128)(2,1)S(1)} %select_bitcast_fusion.3), channel_id=1, source_target_pairs={{0,4},{4,8},{8,12},{12,16},{16,20},{20,24},{24,28},{28,32},{32,36}... | collective-permute-start | bytes 98312 | tf_op jit(solution)/shard_map/ppermute | solution.py:12
  55.0 7.0 %collective-permute-start.5 = (bf16[64,8,32]{2,0,1:T(8,128)(2,1)S(1)}, bf16[64,8,32]{2,0,1:T(8,128)(2,1)S(1)}, u32[]{:S(2)}, u32[]{:S(2)}) collective-permute-start(bf16[64,8,32]{2,0,1:T(8,128)(2,1)S(1)} %select_bitcast_fusion.2), channel_id=1, source_target_pairs={{4,0},{8,4},{12,8},{16,12},{20,16},{24,20},{28,24},{32,28},{36,32}... | collective-permute-start | bytes 98312 | tf_op jit(solution)/shard_map/ppermute | solution.py:12
  62.1 1.9 %collective-permute-start.6 = (bf16[64,8,8]{0,1,2:T(8,128)(2,1)S(1)}, bf16[64,8,8]{0,1,2:T(8,128)(2,1)S(1)}, u32[]{:S(2)}, u32[]{:S(2)}) collective-permute-start(bf16[64,8,8]{0,1,2:T(8,128)(2,1)S(1)} %select_bitcast_fusion.11), channel_id=1, source_target_pairs={{0,8},{4,12},{8,16},{12,20},{16,24},{20,28},{24,32},{28,36},{32,40... | collective-permute-start | bytes 24584 | tf_op jit(solution)/shard_map/ppermute | solution.py:12
  64.1 7.2 %collective-permute-start.7 = (bf16[64,8,8]{0,1,2:T(8,128)(2,1)S(1)}, bf16[64,8,8]{0,1,2:T(8,128)(2,1)S(1)}, u32[]{:S(2)}, u32[]{:S(2)}) collective-permute-start(bf16[64,8,8]{0,1,2:T(8,128)(2,1)S(1)} %select_bitcast_fusion.10), channel_id=1, source_target_pairs={{8,0},{12,4},{16,8},{20,12},{24,16},{28,20},{32,24},{36,28},{40,32... | collective-permute-start | bytes 24584 | tf_op jit(solution)/shard_map/ppermute | solution.py:12
  71.4 12.0 %all_gather.10 = bf16[64,8,32]{0,1,2:T(8,128)(2,1)S(1)} all-gather(bf16[64,8,8]{0,1,2:T(8,128)(2,1)S(1)} %select_bitcast_fusion.9), channel_id=1, replica_groups=mesh['dom'=128,'sub'=4] {'sub'}, dimensions={2}, use_global_device_ids=true | all-gather | bytes 40960 | tf_op jit(solution)/shard_map/all_gather | solution.py:64
  84.5 0.7 gather_fusion.18
  85.2 0.7 gather_fusion.19
  85.9 0.7 gather_fusion.20
  86.5 0.7 gather_fusion.21
  87.2 0.7 gather_fusion.22
  87.9 0.7 gather_fusion.23
  93.6 0.6 gather_fusion.24
  94.2 0.6 gather_fusion.25
  97.1 1.9 %collective-permute-start.8 = (bf16[64,8,32]{2,0,1:T(8,128)(2,1)S(1)}, bf16[64,8,32]{2,0,1:T(8,128)(2,1)S(1)}, u32[]{:S(2)}, u32[]{:S(2)}) collective-permute-start(bf16[64,8,32]{2,0,1:T(8,128)(2,1)S(1)} %select_bitcast_fusion.1), channel_id=1, source_target_pairs={{0,4},{4,8},{8,12},{12,16},{16,20},{20,24},{24,28},{28,32},{32,36}... | collective-permute-start | bytes 98312 | tf_op jit(solution)/shard_map/ppermute | solution.py:12
  99.2 7.0 %collective-permute-start.9 = (bf16[64,8,32]{2,0,1:T(8,128)(2,1)S(1)}, bf16[64,8,32]{2,0,1:T(8,128)(2,1)S(1)}, u32[]{:S(2)}, u32[]{:S(2)}) collective-permute-start(bf16[64,8,32]{2,0,1:T(8,128)(2,1)S(1)} %select_bitcast_fusion), channel_id=1, source_target_pairs={{4,0},{8,4},{12,8},{16,12},{20,16},{24,20},{28,24},{32,28},{36,32}... | collective-permute-start | bytes 98312 | tf_op jit(solution)/shard_map/ppermute | solution.py:12
  106.3 1.9 %collective-permute-start.10 = (bf16[64,8,8]{0,1,2:T(8,128)(2,1)S(1)}, bf16[64,8,8]{0,1,2:T(8,128)(2,1)S(1)}, u32[]{:S(2)}, u32[]{:S(2)}) collective-permute-start(bf16[64,8,8]{0,1,2:T(8,128)(2,1)S(1)} %select_bitcast_fusion.8), channel_id=1, source_target_pairs={{0,8},{4,12},{8,16},{12,20},{16,24},{20,28},{24,32},{28,36},{32,40... | collective-permute-start | bytes 24584 | tf_op jit(solution)/shard_map/ppermute | solution.py:12
  108.3 7.2 %collective-permute-start.11 = (bf16[64,8,8]{0,1,2:T(8,128)(2,1)S(1)}, bf16[64,8,8]{0,1,2:T(8,128)(2,1)S(1)}, u32[]{:S(2)}, u32[]{:S(2)}) collective-permute-start(bf16[64,8,8]{0,1,2:T(8,128)(2,1)S(1)} %select_bitcast_fusion.7), channel_id=1, source_target_pairs={{8,0},{12,4},{16,8},{20,12},{24,16},{28,20},{32,24},{36,28},{40,32... | collective-permute-start | bytes 24584 | tf_op jit(solution)/shard_map/ppermute | solution.py:12
  115.6 11.9 %all_gather.11 = bf16[64,8,32]{0,1,2:T(8,128)(2,1)S(1)} all-gather(bf16[64,8,8]{0,1,2:T(8,128)(2,1)S(1)} %select_bitcast_fusion.6), channel_id=1, replica_groups=mesh['dom'=128,'sub'=4] {'sub'}, dimensions={2}, use_global_device_ids=true | all-gather | bytes 40960 | tf_op jit(solution)/shard_map/all_gather | solution.py:64
  128.5 0.7 gather_fusion.30
  129.2 0.7 gather_fusion.29
  129.9 0.7 gather_fusion.32
  130.6 0.7 gather_fusion.31
  131.3 0.7 gather_fusion.34
  132.0 0.7 gather_fusion.33
  137.9 3.1 %collective-permute-start.12 = (bf16[64,8,16]{2,0,1:T(8,128)(2,1)S(1)}, bf16[64,8,16]{2,0,1:T(8,128)(2,1)S(1)}, u32[]{:S(2)}, u32[]{:S(2)}) collective-permute-start(bf16[64,8,16]{2,0,1:T(8,128)(2,1)S(1)} %fusion.32), channel_id=1, source_target_pairs={{0,1},{1,0},{2,3},{3,2},{4,5},{5,4},{6,7},{7,6},{8,9},{9,8},{10,11... | collective-permute-start | bytes 49160 | tf_op jit(solution)/shard_map/ppermute | solution.py:22
  140.9 0.9 copy.358
  141.8 2.9 %collective-permute-done.12 = bf16[64,8,16]{2,0,1:T(8,128)(2,1)S(1)} collective-permute-done((bf16[64,8,16]{2,0,1:T(8,128)(2,1)S(1)}, bf16[64,8,16]{2,0,1:T(8,128)(2,1)S(1)}, u32[]{:S(2)}, u32[]{:S(2)}) %collective-permute-start.12) | collective-permute-done | bytes 16416 | tf_op jit(solution)/shard_map/ppermute | solution.py:22
  145.1 0.8 gather_fusion.1
  146.3 0.9 copy.357
  (225 shorter events, 27.2 us)
Async XLA Ops:
  0.6 145.4 %copy-start = (bf16[64,64]{1,0:T(8,128)(2,1)S(1)}, bf16[64,64]{1,0:T(8,128)(2,1)}, u32[]{:S(2)}) copy-start(bf16[64,64]{1,0:T(8,128)(2,1)} %param.25) | copy-start | bytes 24580
  0.6 1.9 %copy-start.8 = (s32[2,32]{1,0:T(2,128)S(1)}, s32[2,32]{1,0:T(2,128)}, u32[]{:S(2)}) copy-start(s32[2,32]{1,0:T(2,128)} %param.29) | copy-start | bytes 772
  3.2 9.9 %copy-start.9 = (s32[2,8]{1,0:T(2,128)S(1)}, s32[2,8]{1,0:T(2,128)}, u32[]{:S(2)}) copy-start(s32[2,8]{1,0:T(2,128)} %param.30) | copy-start | bytes 196
  3.3 34.9 %collective-permute-start = (bf16[64,8,32]{2,0,1:T(8,128)(2,1)S(1)}, bf16[64,8,32]{2,0,1:T(8,128)(2,1)S(1)}, u32[]{:S(2)}, u32[]{:S(2)}) collective-permute-start(bf16[64,8,32]{2,0,1:T(8,128)(2,1)S(1)} %select_bitcast_fusion.5), channel_id=1, source_target_pairs={{0,4},{4,8},{8,12},{12,16},{16,20},{20,24},{24,28},{28,32},{32,36}... | collective-permute-start | bytes 98312 | tf_op jit(solution)/shard_map/ppermute | solution.py:12
  5.9 17.7 %copy-start.10 = (s32[8]{0:T(128)S(1)}, s32[8]{0:T(128)}, u32[]{:S(2)}) copy-start(s32[8]{0:T(128)} %param.31) | copy-start | bytes 100
  5.9 17.7 %copy-start.11 = (s32[16]{0:T(128)S(1)}, s32[16]{0:T(128)}, u32[]{:S(2)}) copy-start(s32[16]{0:T(128)} %param.33) | copy-start | bytes 196
  5.9 17.7 %copy-start.12 = (s32[128]{0:T(128)S(1)}, s32[128]{0:T(128)}, u32[]{:S(2)}) copy-start(s32[128]{0:T(128)} %param.32) | copy-start | bytes 1540
  6.1 32.2 %collective-permute-start.1 = (bf16[64,8,32]{2,0,1:T(8,128)(2,1)S(1)}, bf16[64,8,32]{2,0,1:T(8,128)(2,1)S(1)}, u32[]{:S(2)}, u32[]{:S(2)}) collective-permute-start(bf16[64,8,32]{2,0,1:T(8,128)(2,1)S(1)} %select_bitcast_fusion.4), channel_id=1, source_target_pairs={{4,0},{8,4},{12,8},{16,12},{20,16},{24,20},{28,24},{32,28},{36,32}... | collective-permute-start | bytes 98312 | tf_op jit(solution)/shard_map/ppermute | solution.py:12
  13.7 24.2 %collective-permute-start.2 = (bf16[64,8,8]{0,1,2:T(8,128)(2,1)S(1)}, bf16[64,8,8]{0,1,2:T(8,128)(2,1)S(1)}, u32[]{:S(2)}, u32[]{:S(2)}) collective-permute-start(bf16[64,8,8]{0,1,2:T(8,128)(2,1)S(1)} %select_bitcast_fusion.14), channel_id=1, source_target_pairs={{0,8},{4,12},{8,16},{12,20},{16,24},{20,28},{24,32},{28,36},{32,40... | collective-permute-start | bytes 24584 | tf_op jit(solution)/shard_map/ppermute | solution.py:12
  16.3 21.8 %collective-permute-start.3 = (bf16[64,8,8]{0,1,2:T(8,128)(2,1)S(1)}, bf16[64,8,8]{0,1,2:T(8,128)(2,1)S(1)}, u32[]{:S(2)}, u32[]{:S(2)}) collective-permute-start(bf16[64,8,8]{0,1,2:T(8,128)(2,1)S(1)} %select_bitcast_fusion.13), channel_id=1, source_target_pairs={{8,0},{12,4},{16,8},{20,12},{24,16},{28,20},{32,24},{36,28},{40,32... | collective-permute-start | bytes 24584 | tf_op jit(solution)/shard_map/ppermute | solution.py:12
  23.7 0.8 copy-start.4
  23.7 0.8 copy-start.6
  23.7 1.3 copy-start.7
  23.7 1.4 copy-start.3
  23.8 1.4 copy-start.5
  46.7 1.0 copy-start.1
  48.0 1.0 copy-start.2
  52.9 30.9 %collective-permute-start.4 = (bf16[64,8,32]{2,0,1:T(8,128)(2,1)S(1)}, bf16[64,8,32]{2,0,1:T(8,128)(2,1)S(1)}, u32[]{:S(2)}, u32[]{:S(2)}) collective-permute-start(bf16[64,8,32]{2,0,1:T(8,128)(2,1)S(1)} %select_bitcast_fusion.3), channel_id=1, source_target_pairs={{0,4},{4,8},{8,12},{12,16},{16,20},{20,24},{24,28},{28,32},{32,36}... | collective-permute-start | bytes 98312 | tf_op jit(solution)/shard_map/ppermute | solution.py:12
  55.0 28.9 %collective-permute-start.5 = (bf16[64,8,32]{2,0,1:T(8,128)(2,1)S(1)}, bf16[64,8,32]{2,0,1:T(8,128)(2,1)S(1)}, u32[]{:S(2)}, u32[]{:S(2)}) collective-permute-start(bf16[64,8,32]{2,0,1:T(8,128)(2,1)S(1)} %select_bitcast_fusion.2), channel_id=1, source_target_pairs={{4,0},{8,4},{12,8},{16,12},{20,16},{24,20},{28,24},{32,28},{36,32}... | collective-permute-start | bytes 98312 | tf_op jit(solution)/shard_map/ppermute | solution.py:12
  62.1 21.5 %collective-permute-start.6 = (bf16[64,8,8]{0,1,2:T(8,128)(2,1)S(1)}, bf16[64,8,8]{0,1,2:T(8,128)(2,1)S(1)}, u32[]{:S(2)}, u32[]{:S(2)}) collective-permute-start(bf16[64,8,8]{0,1,2:T(8,128)(2,1)S(1)} %select_bitcast_fusion.11), channel_id=1, source_target_pairs={{0,8},{4,12},{8,16},{12,20},{16,24},{20,28},{24,32},{28,36},{32,40... | collective-permute-start | bytes 24584 | tf_op jit(solution)/shard_map/ppermute | solution.py:12
  64.1 19.6 %collective-permute-start.7 = (bf16[64,8,8]{0,1,2:T(8,128)(2,1)S(1)}, bf16[64,8,8]{0,1,2:T(8,128)(2,1)S(1)}, u32[]{:S(2)}, u32[]{:S(2)}) collective-permute-start(bf16[64,8,8]{0,1,2:T(8,128)(2,1)S(1)} %select_bitcast_fusion.10), channel_id=1, source_target_pairs={{8,0},{12,4},{16,8},{20,12},{24,16},{28,20},{32,24},{36,28},{40,32... | collective-permute-start | bytes 24584 | tf_op jit(solution)/shard_map/ppermute | solution.py:12
  97.1 30.8 %collective-permute-start.8 = (bf16[64,8,32]{2,0,1:T(8,128)(2,1)S(1)}, bf16[64,8,32]{2,0,1:T(8,128)(2,1)S(1)}, u32[]{:S(2)}, u32[]{:S(2)}) collective-permute-start(bf16[64,8,32]{2,0,1:T(8,128)(2,1)S(1)} %select_bitcast_fusion.1), channel_id=1, source_target_pairs={{0,4},{4,8},{8,12},{12,16},{16,20},{20,24},{24,28},{28,32},{32,36}... | collective-permute-start | bytes 98312 | tf_op jit(solution)/shard_map/ppermute | solution.py:12
  99.2 28.7 %collective-permute-start.9 = (bf16[64,8,32]{2,0,1:T(8,128)(2,1)S(1)}, bf16[64,8,32]{2,0,1:T(8,128)(2,1)S(1)}, u32[]{:S(2)}, u32[]{:S(2)}) collective-permute-start(bf16[64,8,32]{2,0,1:T(8,128)(2,1)S(1)} %select_bitcast_fusion), channel_id=1, source_target_pairs={{4,0},{8,4},{12,8},{16,12},{20,16},{24,20},{28,24},{32,28},{36,32}... | collective-permute-start | bytes 98312 | tf_op jit(solution)/shard_map/ppermute | solution.py:12
  106.3 21.3 %collective-permute-start.10 = (bf16[64,8,8]{0,1,2:T(8,128)(2,1)S(1)}, bf16[64,8,8]{0,1,2:T(8,128)(2,1)S(1)}, u32[]{:S(2)}, u32[]{:S(2)}) collective-permute-start(bf16[64,8,8]{0,1,2:T(8,128)(2,1)S(1)} %select_bitcast_fusion.8), channel_id=1, source_target_pairs={{0,8},{4,12},{8,16},{12,20},{16,24},{20,28},{24,32},{28,36},{32,40... | collective-permute-start | bytes 24584 | tf_op jit(solution)/shard_map/ppermute | solution.py:12
  108.3 19.5 %collective-permute-start.11 = (bf16[64,8,8]{0,1,2:T(8,128)(2,1)S(1)}, bf16[64,8,8]{0,1,2:T(8,128)(2,1)S(1)}, u32[]{:S(2)}, u32[]{:S(2)}) collective-permute-start(bf16[64,8,8]{0,1,2:T(8,128)(2,1)S(1)} %select_bitcast_fusion.7), channel_id=1, source_target_pairs={{8,0},{12,4},{16,8},{20,12},{24,16},{28,20},{32,24},{36,28},{40,32... | collective-permute-start | bytes 24584 | tf_op jit(solution)/shard_map/ppermute | solution.py:12
  137.9 6.9 %collective-permute-start.12 = (bf16[64,8,16]{2,0,1:T(8,128)(2,1)S(1)}, bf16[64,8,16]{2,0,1:T(8,128)(2,1)S(1)}, u32[]{:S(2)}, u32[]{:S(2)}) collective-permute-start(bf16[64,8,16]{2,0,1:T(8,128)(2,1)S(1)} %fusion.32), channel_id=1, source_target_pairs={{0,1},{1,0},{2,3},{3,2},{4,5},{5,4},{6,7},{7,6},{8,9},{9,8},{10,11... | collective-permute-start | bytes 49160 | tf_op jit(solution)/shard_map/ppermute | solution.py:22
where the time goes:
time: 148 us; the launch traced here: 147 us
  starting transfers between devices  57.2 us (39%)
  local copies, waits for them, and re-layouts  39 us (26%)
  blocking collectives  36.1 us (24%)
  matrix products  6.08 us (4%)
  other arithmetic  3.72 us (3%)
  waiting for transfers between devices  2.94 us (2%)
  between operations  2.13 us (1%)
    ppermute x12, starting transfers between devices, from_behind(): return lax.ppermute(array, axis, pairs)  54.1 us
    all_gather x3, blocking collectives, apply_local(): lax.all_gather(jnp.take(field_b, sub_send, axis=2), 'sub', axis=2, tiled=...  36.1 us
    gather x36, local copies, waits for them, and re-layouts, apply_local(): beside = jnp.take(extended, neighbours[face_index], axis=2)  16.1 us
    dot_general x23, matrix products, stack_apply(): product = jnp.dot(wide_blocks, operand, preferred_element_type=jnp.float32)  5.91 us
    concatenate x23, local copies, waits for them, and re-layouts, stack_apply(): jnp.concatenate(pieces, axis=0)  4.08 us
    unnamed x28, local copies, waits for them, and re-layouts  3.7 us
    ppermute x1, starting transfers between devices, partner_2(): return lax.ppermute(block, axis, route)  3.07 us
  transfers between devices with their start and end apart: 13, of which 1 were waited for; matrix products, arithmetic and copies ran while one was open for 4% of the time, Pallas kernels for 0%

commit v1 on v0

--- a/solution.py
+++ b/solution.py
@@ -61,7 +61,11 @@
         from_above = from_behind(down_near, "dom", -1)
         far_below = from_behind(up_far, "dom", 2)
         far_above = from_behind(down_far, "dom", -2)
-        side_rows = lax.all_gather(jnp.take(field_b, sub_send, axis=2), "sub", axis=2, tiled=True)
+        view = jnp.take(field_b, sub_send, axis=2)
+        newest = tuple((view for _ in range(lax.axis_size("sub"))))
+        e_next = jnp.stack(newest, 0)
+        mid_arr = lax.all_to_all(e_next, "sub", 0, 0)
+        side_rows = jnp.concatenate(mid_arr, 2)
         extended = jnp.concatenate(
             [field_b, from_below, from_above, far_below, far_above, side_rows], axis=2
         )

time: 148 us -> 129 us (0.87)
  the two profiles are of different devices: /device:TPU:256 before, /device:TPU:251 now
where the time goes in v1:
time: 129 us; the launch traced here: 128 us
  starting transfers between devices  57.4 us (44%)
  local copies, waits for them, and re-layouts  41.7 us (32%)
  waiting for transfers between devices  16.8 us (13%)
  matrix products  6.09 us (5%)
  other arithmetic  3.72 us (3%)
  between operations  2.15 us (2%)
    ppermute x12, starting transfers between devices, from_behind(): return lax.ppermute(array, axis, pairs)  42.5 us
    gather x36, local copies, waits for them, and re-layouts, apply_local(): beside = jnp.take(extended, neighbours[face_index], axis=2)  16 us
    all_to_all x3, starting transfers between devices, apply_local(): mid_arr = lax.all_to_all(e_next, 'sub', 0, 0)  12.9 us
    ppermute x12, waiting for transfers between devices, from_behind(): return lax.ppermute(array, axis, pairs)  11.7 us
    unnamed x37, local copies, waits for them, and re-layouts  6.41 us
    dot_general x23, matrix products, stack_apply(): product = jnp.dot(wide_blocks, operand, preferred_element_type=jnp.float32)  5.92 us
    concatenate x23, local copies, waits for them, and re-layouts, stack_apply(): jnp.concatenate(pieces, axis=0)  4.08 us
    ppermute x1, waiting for transfers between devices, partner_2(): return lax.ppermute(block, axis, route)  2.91 us
  transfers between devices with their start and end apart: 16, of which 5 were waited for; matrix products, arithmetic and copies ran while one was open for 7% of the time, Pallas kernels for 0%

profile of v1, /device:TPU:251, one launch (start us, length us, event | category | flops | bytes accessed | tf_op | source)
XLA Modules:
  0.0 127.8 jit_solution(15546771017347738594)
XLA Ops:
  1.3 1.0 broadcast_select_fusion.27
  3.3 5.0 %collective-permute-start = (bf16[64,8,32]{2,0,1:T(8,128)(2,1)S(1)}, bf16[64,8,32]{2,0,1:T(8,128)(2,1)S(1)}, u32[]{:S(2)}, u32[]{:S(2)}) collective-permute-start(bf16[64,8,32]{2,0,1:T(8,128)(2,1)S(1)} %select_bitcast_fusion.5), channel_id=1, source_target_pairs={{0,4},{4,8},{8,12},{12,16},{16,20},{20,24},{24,28},{28,32},{32,36}... | collective-permute-start | bytes 98312 | tf_op jit(solution)/shard_map/ppermute | solution.py:12
  9.1 1.9 %collective-permute-start.1 = (bf16[64,8,32]{2,0,1:T(8,128)(2,1)S(1)}, bf16[64,8,32]{2,0,1:T(8,128)(2,1)S(1)}, u32[]{:S(2)}, u32[]{:S(2)}) collective-permute-start(bf16[64,8,32]{2,0,1:T(8,128)(2,1)S(1)} %select_bitcast_fusion.4), channel_id=1, source_target_pairs={{4,0},{8,4},{12,8},{16,12},{20,16},{24,20},{28,24},{32,28},{36,32}... | collective-permute-start | bytes 98312 | tf_op jit(solution)/shard_map/ppermute | solution.py:12
  11.7 3.2 %collective-permute-start.2 = (bf16[64,8,8]{0,1,2:T(8,128)(2,1)S(1)}, bf16[64,8,8]{0,1,2:T(8,128)(2,1)S(1)}, u32[]{:S(2)}, u32[]{:S(2)}) collective-permute-start(bf16[64,8,8]{0,1,2:T(8,128)(2,1)S(1)} %select_bitcast_fusion.14), channel_id=1, source_target_pairs={{0,8},{4,12},{8,16},{12,20},{16,24},{20,28},{24,32},{28,36},{32,40... | collective-permute-start | bytes 24584 | tf_op jit(solution)/shard_map/ppermute | solution.py:12
  15.6 2.1 %collective-permute-start.3 = (bf16[64,8,8]{0,1,2:T(8,128)(2,1)S(1)}, bf16[64,8,8]{0,1,2:T(8,128)(2,1)S(1)}, u32[]{:S(2)}, u32[]{:S(2)}) collective-permute-start(bf16[64,8,8]{0,1,2:T(8,128)(2,1)S(1)} %select_bitcast_fusion.13), channel_id=1, source_target_pairs={{8,0},{12,4},{16,8},{20,12},{24,16},{28,20},{32,24},{36,28},{40,32... | collective-permute-start | bytes 24584 | tf_op jit(solution)/shard_map/ppermute | solution.py:12
  18.4 0.7 reshape.730
  19.1 4.3 %all-to-all-start = ((bf16[4,2,2048]{2,1,0:T(2,128)(2,1)}), bf16[4,2,2048]{2,1,0:T(2,128)(2,1)S(1)}, u32[]{:S(2)}, u32[]{:S(2)}) async-start(bf16[4,2,2048]{2,1,0:T(2,128)(2,1)} %reshape.730), calls=%async_computation | async-start | bytes 65536 | tf_op jit(solution)/shard_map/all_to_all | solution.py:67
  25.1 1.4 %all-to-all-done = bf16[4,2,2048]{2,1,0:T(2,128)(2,1)S(1)} async-done(((bf16[4,2,2048]{2,1,0:T(2,128)(2,1)}), bf16[4,2,2048]{2,1,0:T(2,128)(2,1)S(1)}, u32[]{:S(2)}, u32[]{:S(2)}) %all-to-all-start) | async-done | bytes 32800 | tf_op jit(solution)/shard_map/all_to_all | solution.py:67
  27.4 0.7 gather_fusion.7
  28.5 0.7 gather_fusion.8
  29.7 0.7 gather_fusion.9
  30.8 0.7 gather_fusion.10
  32.0 0.7 gather_fusion.11
  33.1 0.7 gather_fusion.12
  35.6 0.7 copy-done.1
  36.8 0.7 copy-done.2
  41.5 12.3 %collective-permute-start.4 = (bf16[64,8,32]{2,0,1:T(8,128)(2,1)S(1)}, bf16[64,8,32]{2,0,1:T(8,128)(2,1)S(1)}, u32[]{:S(2)}, u32[]{:S(2)}) collective-permute-start(bf16[64,8,32]{2,0,1:T(8,128)(2,1)S(1)} %select_bitcast_fusion.3), channel_id=1, source_target_pairs={{0,4},{4,8},{8,12},{12,16},{16,20},{20,24},{24,28},{28,32},{32,36}... | collective-permute-start | bytes 98312 | tf_op jit(solution)/shard_map/ppermute | solution.py:12
  54.0 1.9 %collective-permute-start.6 = (bf16[64,8,8]{0,1,2:T(8,128)(2,1)S(1)}, bf16[64,8,8]{0,1,2:T(8,128)(2,1)S(1)}, u32[]{:S(2)}, u32[]{:S(2)}) collective-permute-start(bf16[64,8,8]{0,1,2:T(8,128)(2,1)S(1)} %select_bitcast_fusion.11), channel_id=1, source_target_pairs={{0,8},{4,12},{8,16},{12,20},{16,24},{20,28},{24,32},{28,36},{32,40... | collective-permute-start | bytes 24584 | tf_op jit(solution)/shard_map/ppermute | solution.py:12
  56.0 3.4 %collective-permute-start.7 = (bf16[64,8,8]{0,1,2:T(8,128)(2,1)S(1)}, bf16[64,8,8]{0,1,2:T(8,128)(2,1)S(1)}, u32[]{:S(2)}, u32[]{:S(2)}) collective-permute-start(bf16[64,8,8]{0,1,2:T(8,128)(2,1)S(1)} %select_bitcast_fusion.10), channel_id=1, source_target_pairs={{8,0},{12,4},{16,8},{20,12},{24,16},{28,20},{32,24},{36,28},{40,32... | collective-permute-start | bytes 24584 | tf_op jit(solution)/shard_map/ppermute | solution.py:12
  59.5 0.7 reshape.732
  60.2 4.4 %all-to-all-start.1 = ((bf16[4,2,2048]{2,1,0:T(2,128)(2,1)}), bf16[4,2,2048]{2,1,0:T(2,128)(2,1)S(1)}, u32[]{:S(2)}, u32[]{:S(2)}) async-start(bf16[4,2,2048]{2,1,0:T(2,128)(2,1)} %reshape.732), calls=%async_computation.1 | async-start | bytes 65536 | tf_op jit(solution)/shard_map/all_to_all | solution.py:67
  64.7 2.1 %collective-permute-start.5 = (bf16[64,8,32]{2,0,1:T(8,128)(2,1)S(1)}, bf16[64,8,32]{2,0,1:T(8,128)(2,1)S(1)}, u32[]{:S(2)}, u32[]{:S(2)}) collective-permute-start(bf16[64,8,32]{2,0,1:T(8,128)(2,1)S(1)} %select_bitcast_fusion.2), channel_id=1, source_target_pairs={{4,0},{8,4},{12,8},{16,12},{20,16},{24,20},{28,24},{32,28},{36,32}... | collective-permute-start | bytes 98312 | tf_op jit(solution)/shard_map/ppermute | solution.py:12
  67.1 0.7 all-to-all-done.1
  68.0 6.2 %collective-permute-done.5 = bf16[64,8,32]{2,0,1:T(8,128)(2,1)S(1)} collective-permute-done((bf16[64,8,32]{2,0,1:T(8,128)(2,1)S(1)}, bf16[64,8,32]{2,0,1:T(8,128)(2,1)S(1)}, u32[]{:S(2)}, u32[]{:S(2)}) %collective-permute-start.5) | collective-permute-done | bytes 32800 | tf_op jit(solution)/shard_map/ppermute | solution.py:12
  74.8 0.7 gather_fusion.18
  75.5 0.7 gather_fusion.19
  76.2 0.7 gather_fusion.20
  76.9 0.7 gather_fusion.21
  77.6 0.7 gather_fusion.22
  78.3 0.7 gather_fusion.23
  87.5 1.9 %collective-permute-start.8 = (bf16[64,8,32]{2,0,1:T(8,128)(2,1)S(1)}, bf16[64,8,32]{2,0,1:T(8,128)(2,1)S(1)}, u32[]{:S(2)}, u32[]{:S(2)}) collective-permute-start(bf16[64,8,32]{2,0,1:T(8,128)(2,1)S(1)} %select_bitcast_fusion.1), channel_id=1, source_target_pairs={{0,4},{4,8},{8,12},{12,16},{16,20},{20,24},{24,28},{28,32},{32,36}... | collective-permute-start | bytes 98312 | tf_op jit(solution)/shard_map/ppermute | solution.py:12
  89.6 1.9 %collective-permute-start.10 = (bf16[64,8,8]{0,1,2:T(8,128)(2,1)S(1)}, bf16[64,8,8]{0,1,2:T(8,128)(2,1)S(1)}, u32[]{:S(2)}, u32[]{:S(2)}) collective-permute-start(bf16[64,8,8]{0,1,2:T(8,128)(2,1)S(1)} %select_bitcast_fusion.8), channel_id=1, source_target_pairs={{0,8},{4,12},{8,16},{12,20},{16,24},{20,28},{24,32},{28,36},{32,40... | collective-permute-start | bytes 24584 | tf_op jit(solution)/shard_map/ppermute | solution.py:12
  91.6 3.3 %collective-permute-start.11 = (bf16[64,8,8]{0,1,2:T(8,128)(2,1)S(1)}, bf16[64,8,8]{0,1,2:T(8,128)(2,1)S(1)}, u32[]{:S(2)}, u32[]{:S(2)}) collective-permute-start(bf16[64,8,8]{0,1,2:T(8,128)(2,1)S(1)} %select_bitcast_fusion.7), channel_id=1, source_target_pairs={{8,0},{12,4},{16,8},{20,12},{24,16},{28,20},{32,24},{36,28},{40,32... | collective-permute-start | bytes 24584 | tf_op jit(solution)/shard_map/ppermute | solution.py:12
  95.1 0.7 reshape.734
  95.8 4.2 %all-to-all-start.2 = ((bf16[4,2,2048]{2,1,0:T(2,128)(2,1)}), bf16[4,2,2048]{2,1,0:T(2,128)(2,1)S(1)}, u32[]{:S(2)}, u32[]{:S(2)}) async-start(bf16[4,2,2048]{2,1,0:T(2,128)(2,1)} %reshape.734), calls=%async_computation.2 | async-start | bytes 65536 | tf_op jit(solution)/shard_map/all_to_all | solution.py:67
  100.1 3.5 %collective-permute-start.9 = (bf16[64,8,32]{2,0,1:T(8,128)(2,1)S(1)}, bf16[64,8,32]{2,0,1:T(8,128)(2,1)S(1)}, u32[]{:S(2)}, u32[]{:S(2)}) collective-permute-start(bf16[64,8,32]{2,0,1:T(8,128)(2,1)S(1)} %select_bitcast_fusion), channel_id=1, source_target_pairs={{4,0},{8,4},{12,8},{16,12},{20,16},{24,20},{28,24},{32,28},{36,32}... | collective-permute-start | bytes 98312 | tf_op jit(solution)/shard_map/ppermute | solution.py:12
  104.2 5.5 %collective-permute-done.9 = bf16[64,8,32]{2,0,1:T(8,128)(2,1)S(1)} collective-permute-done((bf16[64,8,32]{2,0,1:T(8,128)(2,1)S(1)}, bf16[64,8,32]{2,0,1:T(8,128)(2,1)S(1)}, u32[]{:S(2)}, u32[]{:S(2)}) %collective-permute-start.9) | collective-permute-done | bytes 32800 | tf_op jit(solution)/shard_map/ppermute | solution.py:12
  110.3 0.7 gather_fusion.30
  111.0 0.7 gather_fusion.29
  111.7 0.7 gather_fusion.32
  112.4 0.7 gather_fusion.31
  113.1 0.7 gather_fusion.34
  113.7 0.7 gather_fusion.33
  119.6 1.9 %collective-permute-start.12 = (bf16[64,8,16]{2,0,1:T(8,128)(2,1)S(1)}, bf16[64,8,16]{2,0,1:T(8,128)(2,1)S(1)}, u32[]{:S(2)}, u32[]{:S(2)}) collective-permute-start(bf16[64,8,16]{2,0,1:T(8,128)(2,1)S(1)} %fusion.32), channel_id=1, source_target_pairs={{0,1},{1,0},{2,3},{3,2},{4,5},{5,4},{6,7},{7,6},{8,9},{9,8},{10,11... | collective-permute-start | bytes 49160 | tf_op jit(solution)/shard_map/ppermute | solution.py:22
  121.6 0.9 copy.367
  122.4 2.9 %collective-permute-done.12 = bf16[64,8,16]{2,0,1:T(8,128)(2,1)S(1)} collective-permute-done((bf16[64,8,16]{2,0,1:T(8,128)(2,1)S(1)}, bf16[64,8,16]{2,0,1:T(8,128)(2,1)S(1)}, u32[]{:S(2)}, u32[]{:S(2)}) %collective-permute-start.12) | collective-permute-done | bytes 16416 | tf_op jit(solution)/shard_map/ppermute | solution.py:22
  125.7 0.8 gather_fusion.1
  126.9 0.9 copy.366
  (243 shorter events, 32.0 us)
Async XLA Ops:
  0.6 126.1 %copy-start = (bf16[64,64]{1,0:T(8,128)(2,1)S(1)}, bf16[64,64]{1,0:T(8,128)(2,1)}, u32[]{:S(2)}) copy-start(bf16[64,64]{1,0:T(8,128)(2,1)} %param.25) | copy-start | bytes 24580
  0.6 1.9 %copy-start.8 = (s32[2,32]{1,0:T(2,128)S(1)}, s32[2,32]{1,0:T(2,128)}, u32[]{:S(2)}) copy-start(s32[2,32]{1,0:T(2,128)} %param.29) | copy-start | bytes 772
  3.2 7.9 %copy-start.9 = (s32[2,8]{1,0:T(2,128)S(1)}, s32[2,8]{1,0:T(2,128)}, u32[]{:S(2)}) copy-start(s32[2,8]{1,0:T(2,128)} %param.30) | copy-start | bytes 196
  3.3 23.5 %collective-permute-start = (bf16[64,8,32]{2,0,1:T(8,128)(2,1)S(1)}, bf16[64,8,32]{2,0,1:T(8,128)(2,1)S(1)}, u32[]{:S(2)}, u32[]{:S(2)}) collective-permute-start(bf16[64,8,32]{2,0,1:T(8,128)(2,1)S(1)} %select_bitcast_fusion.5), channel_id=1, source_target_pairs={{0,4},{4,8},{8,12},{12,16},{16,20},{20,24},{24,28},{28,32},{32,36}... | collective-permute-start | bytes 98312 | tf_op jit(solution)/shard_map/ppermute | solution.py:12
  8.9 8.8 %copy-start.10 = (s32[8]{0:T(128)S(1)}, s32[8]{0:T(128)}, u32[]{:S(2)}) copy-start(s32[8]{0:T(128)} %param.31) | copy-start | bytes 100
  9.1 17.7 %collective-permute-start.1 = (bf16[64,8,32]{2,0,1:T(8,128)(2,1)S(1)}, bf16[64,8,32]{2,0,1:T(8,128)(2,1)S(1)}, u32[]{:S(2)}, u32[]{:S(2)}) collective-permute-start(bf16[64,8,32]{2,0,1:T(8,128)(2,1)S(1)} %select_bitcast_fusion.4), channel_id=1, source_target_pairs={{4,0},{8,4},{12,8},{16,12},{20,16},{24,20},{28,24},{32,28},{36,32}... | collective-permute-start | bytes 98312 | tf_op jit(solution)/shard_map/ppermute | solution.py:12
  11.1 12.3 %copy-start.11 = (s32[16]{0:T(128)S(1)}, s32[16]{0:T(128)}, u32[]{:S(2)}) copy-start(s32[16]{0:T(128)} %param.33) | copy-start | bytes 196
  11.1 12.3 %copy-start.12 = (s32[128]{0:T(128)S(1)}, s32[128]{0:T(128)}, u32[]{:S(2)}) copy-start(s32[128]{0:T(128)} %param.32) | copy-start | bytes 1540
  11.7 13.1 %collective-permute-start.2 = (bf16[64,8,8]{0,1,2:T(8,128)(2,1)S(1)}, bf16[64,8,8]{0,1,2:T(8,128)(2,1)S(1)}, u32[]{:S(2)}, u32[]{:S(2)}) collective-permute-start(bf16[64,8,8]{0,1,2:T(8,128)(2,1)S(1)} %select_bitcast_fusion.14), channel_id=1, source_target_pairs={{0,8},{4,12},{8,16},{12,20},{16,24},{20,28},{24,32},{28,36},{32,40... | collective-permute-start | bytes 24584 | tf_op jit(solution)/shard_map/ppermute | solution.py:12
  15.6 9.4 %collective-permute-start.3 = (bf16[64,8,8]{0,1,2:T(8,128)(2,1)S(1)}, bf16[64,8,8]{0,1,2:T(8,128)(2,1)S(1)}, u32[]{:S(2)}, u32[]{:S(2)}) collective-permute-start(bf16[64,8,8]{0,1,2:T(8,128)(2,1)S(1)} %select_bitcast_fusion.13), channel_id=1, source_target_pairs={{8,0},{12,4},{16,8},{20,12},{24,16},{28,20},{32,24},{36,28},{40,32... | collective-permute-start | bytes 24584 | tf_op jit(solution)/shard_map/ppermute | solution.py:12
  19.1 7.4 %all-to-all-start = ((bf16[4,2,2048]{2,1,0:T(2,128)(2,1)}), bf16[4,2,2048]{2,1,0:T(2,128)(2,1)S(1)}, u32[]{:S(2)}, u32[]{:S(2)}) async-start(bf16[4,2,2048]{2,1,0:T(2,128)(2,1)} %reshape.730), calls=%async_computation | async-start | bytes 65536 | tf_op jit(solution)/shard_map/all_to_all | solution.py:67
  23.5 0.8 copy-start.4
  23.5 0.8 copy-start.6
  23.5 0.8 copy-start.7
  23.5 0.9 copy-start.3
  23.6 1.0 copy-start.5
  35.3 1.0 copy-start.1
  36.5 1.0 copy-start.2
  41.5 26.5 %collective-permute-start.4 = (bf16[64,8,32]{2,0,1:T(8,128)(2,1)S(1)}, bf16[64,8,32]{2,0,1:T(8,128)(2,1)S(1)}, u32[]{:S(2)}, u32[]{:S(2)}) collective-permute-start(bf16[64,8,32]{2,0,1:T(8,128)(2,1)S(1)} %select_bitcast_fusion.3), channel_id=1, source_target_pairs={{0,4},{4,8},{8,12},{12,16},{16,20},{20,24},{24,28},{28,32},{32,36}... | collective-permute-start | bytes 98312 | tf_op jit(solution)/shard_map/ppermute | solution.py:12
  54.0 12.8 %collective-permute-start.6 = (bf16[64,8,8]{0,1,2:T(8,128)(2,1)S(1)}, bf16[64,8,8]{0,1,2:T(8,128)(2,1)S(1)}, u32[]{:S(2)}, u32[]{:S(2)}) collective-permute-start(bf16[64,8,8]{0,1,2:T(8,128)(2,1)S(1)} %select_bitcast_fusion.11), channel_id=1, source_target_pairs={{0,8},{4,12},{8,16},{12,20},{16,24},{20,28},{24,32},{28,36},{32,40... | collective-permute-start | bytes 24584 | tf_op jit(solution)/shard_map/ppermute | solution.py:12
  56.0 10.9 %collective-permute-start.7 = (bf16[64,8,8]{0,1,2:T(8,128)(2,1)S(1)}, bf16[64,8,8]{0,1,2:T(8,128)(2,1)S(1)}, u32[]{:S(2)}, u32[]{:S(2)}) collective-permute-start(bf16[64,8,8]{0,1,2:T(8,128)(2,1)S(1)} %select_bitcast_fusion.10), channel_id=1, source_target_pairs={{8,0},{12,4},{16,8},{20,12},{24,16},{28,20},{32,24},{36,28},{40,32... | collective-permute-start | bytes 24584 | tf_op jit(solution)/shard_map/ppermute | solution.py:12
  60.2 7.5 %all-to-all-start.1 = ((bf16[4,2,2048]{2,1,0:T(2,128)(2,1)}), bf16[4,2,2048]{2,1,0:T(2,128)(2,1)S(1)}, u32[]{:S(2)}, u32[]{:S(2)}) async-start(bf16[4,2,2048]{2,1,0:T(2,128)(2,1)} %reshape.732), calls=%async_computation.1 | async-start | bytes 65536 | tf_op jit(solution)/shard_map/all_to_all | solution.py:67
  64.7 9.6 %collective-permute-start.5 = (bf16[64,8,32]{2,0,1:T(8,128)(2,1)S(1)}, bf16[64,8,32]{2,0,1:T(8,128)(2,1)S(1)}, u32[]{:S(2)}, u32[]{:S(2)}) collective-permute-start(bf16[64,8,32]{2,0,1:T(8,128)(2,1)S(1)} %select_bitcast_fusion.2), channel_id=1, source_target_pairs={{4,0},{8,4},{12,8},{16,12},{20,16},{24,20},{28,24},{32,28},{36,32}... | collective-permute-start | bytes 98312 | tf_op jit(solution)/shard_map/ppermute | solution.py:12
  87.5 16.7 %collective-permute-start.8 = (bf16[64,8,32]{2,0,1:T(8,128)(2,1)S(1)}, bf16[64,8,32]{2,0,1:T(8,128)(2,1)S(1)}, u32[]{:S(2)}, u32[]{:S(2)}) collective-permute-start(bf16[64,8,32]{2,0,1:T(8,128)(2,1)S(1)} %select_bitcast_fusion.1), channel_id=1, source_target_pairs={{0,4},{4,8},{8,12},{12,16},{16,20},{20,24},{24,28},{28,32},{32,36}... | collective-permute-start | bytes 98312 | tf_op jit(solution)/shard_map/ppermute | solution.py:12
  89.6 14.0 %collective-permute-start.10 = (bf16[64,8,8]{0,1,2:T(8,128)(2,1)S(1)}, bf16[64,8,8]{0,1,2:T(8,128)(2,1)S(1)}, u32[]{:S(2)}, u32[]{:S(2)}) collective-permute-start(bf16[64,8,8]{0,1,2:T(8,128)(2,1)S(1)} %select_bitcast_fusion.8), channel_id=1, source_target_pairs={{0,8},{4,12},{8,16},{12,20},{16,24},{20,28},{24,32},{28,36},{32,40... | collective-permute-start | bytes 24584 | tf_op jit(solution)/shard_map/ppermute | solution.py:12
  91.6 12.1 %collective-permute-start.11 = (bf16[64,8,8]{0,1,2:T(8,128)(2,1)S(1)}, bf16[64,8,8]{0,1,2:T(8,128)(2,1)S(1)}, u32[]{:S(2)}, u32[]{:S(2)}) collective-permute-start(bf16[64,8,8]{0,1,2:T(8,128)(2,1)S(1)} %select_bitcast_fusion.7), channel_id=1, source_target_pairs={{8,0},{12,4},{16,8},{20,12},{24,16},{28,20},{32,24},{36,28},{40,32... | collective-permute-start | bytes 24584 | tf_op jit(solution)/shard_map/ppermute | solution.py:12
  95.8 8.1 %all-to-all-start.2 = ((bf16[4,2,2048]{2,1,0:T(2,128)(2,1)}), bf16[4,2,2048]{2,1,0:T(2,128)(2,1)S(1)}, u32[]{:S(2)}, u32[]{:S(2)}) async-start(bf16[4,2,2048]{2,1,0:T(2,128)(2,1)} %reshape.734), calls=%async_computation.2 | async-start | bytes 65536 | tf_op jit(solution)/shard_map/all_to_all | solution.py:67
  100.1 9.6 %collective-permute-start.9 = (bf16[64,8,32]{2,0,1:T(8,128)(2,1)S(1)}, bf16[64,8,32]{2,0,1:T(8,128)(2,1)S(1)}, u32[]{:S(2)}, u32[]{:S(2)}) collective-permute-start(bf16[64,8,32]{2,0,1:T(8,128)(2,1)S(1)} %select_bitcast_fusion), channel_id=1, source_target_pairs={{4,0},{8,4},{12,8},{16,12},{20,16},{24,20},{28,24},{32,28},{36,32}... | collective-permute-start | bytes 98312 | tf_op jit(solution)/shard_map/ppermute | solution.py:12
  119.6 5.7 %collective-permute-start.12 = (bf16[64,8,16]{2,0,1:T(8,128)(2,1)S(1)}, bf16[64,8,16]{2,0,1:T(8,128)(2,1)S(1)}, u32[]{:S(2)}, u32[]{:S(2)}) collective-permute-start(bf16[64,8,16]{2,0,1:T(8,128)(2,1)S(1)} %fusion.32), channel_id=1, source_target_pairs={{0,1},{1,0},{2,3},{3,2},{4,5},{5,4},{6,7},{7,6},{8,9},{9,8},{10,11... | collective-permute-start | bytes 49160 | tf_op jit(solution)/shard_map/ppermute | solution.py:22
